TPU v7x, 32 devices: a whole 2x2x4 slice. The times are simulated.
32 devices in a mesh: group: 2 (over y), seq: 8 (over z, x), tensor: 2 (over core).
Axes of the slice: x: 2, y: 2, z: 4, core: 2. Of those that a mesh axis runs over, the one named last changes fastest.
Arguments:
- streams: bfloat16 [3, 128, 16, 2048], P(None, 'seq', 'group', 'tensor'), parts along dimension 2, may hold values from -6 to 6
- short_taps: float32 [3, 3, 2048], P(None, None, 'tensor'), may hold values from -3 to 3
- long_filters: bfloat16 [2, 128, 8, 2048], P(None, 'seq', None, 'tensor'), may hold values from -0.1875 to 0.1875
- out_grad: bfloat16 [128, 16, 2048], P('seq', 'group', 'tensor'), parts along dimension 1, may hold values from -6 to 6
Outputs:
- layer_out: bfloat16 [128, 16, 2048], P('seq', 'group', 'tensor'), parts along dimension 1
- stream_grads: bfloat16 [3, 128, 16, 2048], P(None, 'seq', 'group', 'tensor'), parts along dimension 2
- tap_grads: float32 [6, 3, 2048], P('group', None, 'tensor'), parts along dimension 0
There are 2 independent parts, one for each index of `group`. A program takes and returns all parts, laid end to end along the dimension named above; an argument that names none is the same for every part. Nothing has to cross between parts.
All inputs are finite; a program needn't handle non-finite values.
Results may differ from a plain program's by a relative error of at most 0.0064.
Values may be sent and summed in bfloat16 or wider, within the bound.
A program may use at most 64 MiB of HBM per device.

v0:
```python
import functools
import math

import jax
import jax.numpy as jnp
import ml_dtypes
import numpy as np
from jax import lax
from jax.experimental import pallas as pl
from jax.experimental.pallas import tpu as pltpu
from jax.sharding import PartitionSpec as P

HIGHEST_PRECISION = lax.Precision.HIGHEST
MESH = pl.DeviceIdType.MESH
LANES = 128
TILE = 256
F32 = jnp.float32
BF16 = jnp.bfloat16


def shifted(value, axis, by):
    count = lax.axis_size(axis)
    return lax.ppermute(value, axis, [(i, (i + by) % count) for i in range(count)])


def complex_product(left_real, left_imag, right_real, right_imag):
    return (
        left_real * right_real - left_imag * right_imag,
        left_real * right_imag + left_imag * right_real,
    )


def conj_product(left_real, left_imag, right_real, right_imag):
    return (
        left_real * right_real + left_imag * right_imag,
        left_real * right_imag - left_imag * right_real,
    )


def local(streams, short_taps, long_filters, out_grad):
    seq_count = lax.axis_size("seq")
    seq_place = lax.axis_index("seq")
    local_rows = streams.shape[1]
    channels = streams.shape[3]
    block_rows = local_rows * seq_count
    full_length = 2 * block_rows * seq_count
    angle_unit = math.pi / full_length
    block_pos = jnp.arange(seq_count, dtype=jnp.int32)
    odd_slots = 2 * block_pos + 1
    local_index = seq_place * local_rows + jnp.arange(local_rows, dtype=jnp.int32)
    row_pos = jnp.arange(block_rows, dtype=jnp.int32)
    start_pos = block_pos[None, :, None] * block_rows + local_index[:, None, None]
    fwd_angle = (start_pos * odd_slots[None, None, :] % (2 * full_length)).astype(
        jnp.float32
    ) * angle_unit
    fwd_table = jnp.stack([jnp.cos(fwd_angle), -jnp.sin(fwd_angle)], axis=-1)
    inner_angle = (row_pos[:, None] * row_pos[None, :] % block_rows).astype(jnp.float32) * (
        2.0 * math.pi / block_rows
    )
    inner_cos = jnp.cos(inner_angle)
    inner_sin = jnp.sin(inner_angle)
    inner_table = jnp.stack(
        [jnp.stack([inner_cos, -inner_sin], axis=-1), jnp.stack([inner_sin, inner_cos], axis=-1)],
        axis=0,
    )
    back_num = (
        row_pos[None, :]
        * (4 * seq_count * row_pos[:, None] + 2 * seq_place + 1)
        % (2 * full_length)
    )
    back_angle = back_num.astype(jnp.float32) * angle_unit
    back_cos = jnp.cos(back_angle)
    back_sin = jnp.sin(back_angle)
    back_table = jnp.stack(
        [jnp.stack([back_cos, back_sin], axis=-1), jnp.stack([-back_sin, back_cos], axis=-1)],
        axis=0,
    )
    outer_angle = (block_pos[:, None] * odd_slots[None, :] % (4 * seq_count)).astype(
        jnp.float32
    ) * (math.pi / (2 * seq_count))
    outer_table = jnp.stack([jnp.cos(outer_angle).T, -jnp.sin(outer_angle).T], axis=0)

    def previous_rows(block):
        edge = shifted(block[:, -1:], "seq", 1)
        rolled = jnp.concatenate([jnp.zeros_like(edge[:, :, :1]), edge[:, :, :-1]], axis=2)
        edge = jnp.where(seq_place == 0, rolled, edge)
        return jnp.concatenate([edge, block[:, :-1]], axis=1)

    def next_rows(block):
        edge = shifted(block[:, :1], "seq", -1)
        rolled = jnp.concatenate([edge[:, :, 1:], jnp.zeros_like(edge[:, :, :1])], axis=2)
        edge = jnp.where(seq_place == seq_count - 1, rolled, edge)
        return jnp.concatenate([block[:, 1:], edge], axis=1)

    def spectra(signals):
        count = signals.shape[0]
        twisted = jnp.einsum("simc,imjr->srijc", signals, fwd_table, precision=HIGHEST_PRECISION)
        slotted = lax.all_to_all(twisted, "seq", split_axis=3, concat_axis=2, tiled=True)
        slotted = slotted.reshape(count, 2, block_rows, channels)
        spec = jnp.einsum("sric,rikq->sqkc", slotted, inner_table, precision=HIGHEST_PRECISION)
        return (spec[:, 0], spec[:, 1])

    def signals_back(real_spec, imag_spec):
        count = real_spec.shape[0]
        stacked = jnp.stack([real_spec, imag_spec], axis=1)
        turned = jnp.einsum("srkc,rkiq->sqic", stacked, back_table, precision=HIGHEST_PRECISION)
        turned = turned.reshape(count, 2, block_rows, 1, channels)
        parts = lax.all_to_all(turned, "seq", split_axis=2, concat_axis=3, tiled=True)
        rows_out = jnp.einsum("srijc,rjm->simc", parts, outer_table, precision=HIGHEST_PRECISION)
        return rows_out * (2.0 / full_length)

    def tap_weight(index):
        return short_taps[:, index][:, None, None, :]

    prev_one = previous_rows(streams)
    prev_two = previous_rows(prev_one)
    filtered = (
        tap_weight(0) * streams + tap_weight(1) * prev_one + tap_weight(2) * prev_two
    ).astype(jnp.bfloat16)
    value_stream = filtered[0].astype(jnp.float32)
    gate_one = filtered[1].astype(jnp.float32)
    gate_two = filtered[2].astype(jnp.float32)
    filters = long_filters.astype(jnp.float32)
    real_first, imag_first = spectra(jnp.stack([value_stream, filters[0]]))
    product_one = complex_product(real_first[0], imag_first[0], real_first[1], imag_first[1])
    first_conv = signals_back(product_one[0][None], product_one[1][None])[0]
    gated_first = gate_one * first_conv
    real_second, imag_second = spectra(jnp.stack([gated_first, filters[1]]))
    product_two = complex_product(real_second[0], imag_second[0], real_second[1], imag_second[1])
    second_conv = signals_back(product_two[0][None], product_two[1][None])[0]
    layer_out = (gate_two * second_conv).astype(jnp.bfloat16)
    cotangent = out_grad.astype(jnp.float32)
    back_two = cotangent * gate_two
    grad_two = cotangent * second_conv
    real_third, imag_third = spectra(back_two[None])
    filter_two_real, filter_two_imag = (real_second[1], imag_second[1])
    correlated_two = conj_product(filter_two_real, filter_two_imag, real_third[0], imag_third[0])
    grad_gated = signals_back(correlated_two[0][None], correlated_two[1][None])[0]
    grad_one = grad_gated * first_conv
    back_one = grad_gated * gate_one
    real_fourth, imag_fourth = spectra(back_one[None])
    filter_one_real, filter_one_imag = (real_first[1], imag_first[1])
    correlated_one = conj_product(filter_one_real, filter_one_imag, real_fourth[0], imag_fourth[0])
    grad_value = signals_back(correlated_one[0][None], correlated_one[1][None])[0]
    stream_cot = jnp.stack([grad_value, grad_one, grad_two]).astype(jnp.bfloat16)
    next_one = next_rows(stream_cot)
    next_two = next_rows(next_one)
    stream_grads = (
        tap_weight(0) * stream_cot + tap_weight(1) * next_one + tap_weight(2) * next_two
    ).astype(jnp.bfloat16)
    cot_float = stream_cot.astype(jnp.float32)
    tap_terms = jnp.stack(
        [
            jnp.sum(cot_float * streams, axis=(1, 2)),
            jnp.sum(cot_float * prev_one, axis=(1, 2)),
            jnp.sum(cot_float * prev_two, axis=(1, 2)),
        ],
        axis=1,
    )
    tap_total = lax.psum(tap_terms, "seq")
    return (layer_out, stream_grads, tap_total * (1.0 / math.sqrt(block_rows * seq_count)))


def dft_tables(blocks, rows):
    length = blocks * rows
    place = np.arange(length)
    time = (place % blocks) * rows + place // blocks
    half = TILE // 2
    freq = np.arange(length).reshape(-1, half)
    angle = ((2 * freq[:, :, None] + 1) * time[None, None, :] % (4 * length)) * (math.pi / (2 * length))
    table = np.concatenate([np.cos(angle), -np.sin(angle)], axis=1).reshape(2 * length, length)
    return (
        table.astype(ml_dtypes.bfloat16),
        np.ascontiguousarray(table.T / length).astype(ml_dtypes.bfloat16),
    )


FILTER0, FILTER1, VALUE, GATE_TWO, OUT_GRAD, GATE_ONE, SG_ONE, LAYER, SG_TWO, SG_VALUE, TAPS_OUT = range(11)


def kernel(
    seq, blocks, streams, taps, filters, out_grad, fwd_hbm, inv_hbm,
    layer_out, stream_grads, tap_out,
    fwd, inv, xf, sb, og, s32, cot, gates, sig, spec_f, prod, conv, conv2, staged, tap_send,
    send_sem, recv_sem, table_sem,
):
    me = lax.axis_index("seq")
    part = streams.shape[1]
    length = part * seq
    half = TILE // 2
    order = sorted(range(1, seq), key=lambda k: abs(k - seq / 2))

    def peer(k):
        return lax.rem(me + k, seq)

    def lanes(d):
        return pl.ds(pl.multiple_of(d * LANES, LANES), LANES)

    def rows(d):
        return pl.ds(pl.multiple_of(d * part, part), part)

    def remote(slot, k, src, dst):
        return pltpu.make_async_remote_copy(
            src_ref=src, dst_ref=dst, send_sem=send_sem.at[slot, k], recv_sem=recv_sem.at[slot, k],
            device_id={"seq": peer(k)}, device_id_type=MESH,
        )

    def exchange(slot, src_of, dst):
        own = pltpu.make_async_copy(src_of(me), dst, recv_sem.at[slot, 0])
        copies = [remote(slot, k, src_of(peer(k)), dst) for k in order]
        for copy in copies:
            copy.start()
        own.start()
        return own, copies

    def arrive(exchanged):
        own, copies = exchanged
        own.wait()
        for copy in copies:
            copy.wait_recv()

    barrier = pltpu.get_barrier_semaphore()
    for k in range(1, seq):
        pl.semaphore_signal(barrier, inc=1, device_id={"seq": peer(k)}, device_id_type=MESH)
    fwd_copy = pltpu.make_async_copy(fwd_hbm, fwd, table_sem.at[0])
    inv_copy = pltpu.make_async_copy(inv_hbm, inv, table_sem.at[1])
    fwd_copy.start()
    inv_copy.start()
    pl.semaphore_wait(barrier, seq - 1)

    mine = rows(me)
    in_f0 = exchange(FILTER0, lambda d: filters.at[0, :, lanes(d)], xf.at[mine, pl.ds(0, LANES)])
    in_f1 = exchange(FILTER1, lambda d: filters.at[1, :, lanes(d)], xf.at[mine, pl.ds(LANES, LANES)])
    in_v = exchange(VALUE, lambda d: streams.at[0, :, lanes(d)], sb.at[0, mine])
    in_g2 = exchange(GATE_TWO, lambda d: streams.at[2, :, lanes(d)], sb.at[2, mine])
    in_og = exchange(OUT_GRAD, lambda d: out_grad.at[:, lanes(d)], og.at[mine])
    in_g1 = exchange(GATE_ONE, lambda d: streams.at[1, :, lanes(d)], sb.at[1, mine])
    sent = [in_f0, in_f1, in_v, in_g2, in_og, in_g1]

    pad = 2 * blocks
    sub = lax.broadcasted_iota(jnp.int32, (blocks, LANES), 0)

    def tap(s, j):
        return taps[pl.ds(3 * s + j, 1), lanes(me)]

    def chunk(c):
        return pl.ds(pl.multiple_of(c * part, part), part)

    def offset(c, by):
        return pl.ds(pl.multiple_of(c * part + by, blocks), part)

    def widen(s):
        def body(c, carry):
            s32[s, offset(c, pad), :] = sb[s, chunk(c), :].astype(F32)
            return carry

        lax.fori_loop(0, seq, body, 0)
        for step in range(2):
            edge = s32[s, pl.ds(length + step * blocks, blocks), :]
            s32[s, pl.ds(step * blocks, blocks), :] = jnp.where(sub == 0, 0.0, pltpu.roll(edge, 1, 0))

    def filtered(s, c):
        total = tap(s, 0) * s32[s, offset(c, pad), :]
        total = total + tap(s, 1) * s32[s, offset(c, blocks), :]
        total = total + tap(s, 2) * s32[s, offset(c, 0), :]
        return total.astype(BF16)

    def cots(s, c):
        base = [cot[s, offset(c, j * blocks), :] for j in range(3)]
        total = tap(s, 0) * base[0] + tap(s, 1) * base[1] + tap(s, 2) * base[2]
        return total.astype(BF16)

    def close(s):
        for step in range(2):
            edge = cot[s, pl.ds(step * blocks, blocks), :]
            cot[s, pl.ds(length + step * blocks, blocks), :] = jnp.where(
                sub == blocks - 1, 0.0, pltpu.roll(edge, blocks - 1, 0)
            )

    def grads_of(s, slot):
        def body(c, sums):
            staged[slot, chunk(c), :] = cots(s, c)
            now = cot[s, offset(c, 0), :]
            return tuple(
                sums[j]
                + jnp.sum(
                    (now * s32[s, offset(c, pad - j * blocks), :]).reshape(-1, 8, LANES), axis=0
                )
                for j in range(3)
            )

        sums = lax.fori_loop(0, seq, body, tuple(jnp.zeros((8, LANES), F32) for _ in range(3)))
        for j in range(3):
            tap_send[pl.ds(3 * s + j, 1), :] = jnp.sum(sums[j], axis=0, keepdims=True) * (
                1.0 / math.sqrt(length)
            )

    def tile(m):
        return pl.ds(pl.multiple_of(m * TILE, TILE), TILE)

    def forward(m, signals):
        out = jnp.dot(fwd[tile(m), :], signals[...], preferred_element_type=F32)
        return out[:half], out[half:]

    def put(m, col, real, imag):
        prod[pl.ds(pl.multiple_of(m * TILE, TILE), half), col * LANES:(col + 1) * LANES] = real.astype(BF16)
        prod[pl.ds(pl.multiple_of(m * TILE + half, half), half), col * LANES:(col + 1) * LANES] = imag.astype(BF16)

    def spectra_of(m, col):
        cols = slice(col * LANES, (col + 1) * LANES)
        return (
            spec_f[pl.ds(pl.multiple_of(m * TILE, TILE), half), cols],
            spec_f[pl.ds(pl.multiple_of(m * TILE + half, half), half), cols],
        )

    def inverse(into):
        def body(m, carry):
            into[tile(m), :] = jnp.dot(inv[tile(m), :], prod[...], preferred_element_type=F32)
            return carry

        lax.fori_loop(0, length // TILE, body, 0)

    fwd_copy.wait()
    arrive(in_f0)
    arrive(in_f1)

    def filter_body(m, carry):
        spec_f[tile(m), :] = jnp.dot(fwd[tile(m), :], xf[...], preferred_element_type=F32)
        return carry

    lax.fori_loop(0, 2 * length // TILE, filter_body, 0)

    arrive(in_v)
    widen(0)

    def value_body(c, carry):
        sig[chunk(c), 0:LANES] = filtered(0, c)
        return carry

    lax.fori_loop(0, seq, value_body, 0)
    arrive(in_g2)
    widen(2)

    arrive(in_og)

    def back_body(c, carry):
        gate = filtered(2, c)
        gates[1, chunk(c), :] = gate.astype(F32)
        sig[chunk(c), LANES:] = (og[chunk(c), :].astype(F32) * gate.astype(F32)).astype(BF16)
        return carry

    lax.fori_loop(0, seq, back_body, 0)

    def first_body(m, carry):
        real, imag = forward(m, sig)
        f0r, f0i = spectra_of(m, 0)
        f1r, f1i = spectra_of(m, 1)
        vr, vi, br, bi = real[:, :LANES], imag[:, :LANES], real[:, LANES:], imag[:, LANES:]
        put(m, 0, *complex_product(vr, vi, f0r, f0i))
        put(m, 1, *conj_product(f1r, f1i, br, bi))
        return carry

    lax.fori_loop(0, 2 * length // TILE, first_body, 0)
    inv_copy.wait()
    inverse(conv)

    def one_body(c, carry):
        both = conv[chunk(c), :]
        cot[1, offset(c, 0), :] = (both[:, LANES:] * both[:, :LANES]).astype(BF16).astype(F32)
        return carry

    lax.fori_loop(0, seq, one_body, 0)
    close(1)
    arrive(in_g1)
    widen(1)
    grads_of(1, 2)
    out_one = exchange(SG_ONE, lambda d: staged.at[2, rows(d)], stream_grads.at[1, :, lanes(me)])

    def gated_body(c, carry):
        gate = filtered(1, c).astype(F32)
        both = conv[chunk(c), :]
        sig[chunk(c), 0:LANES] = (gate * both[:, :LANES]).astype(BF16)
        sig[chunk(c), LANES:] = (gate * both[:, LANES:]).astype(BF16)
        return carry

    lax.fori_loop(0, seq, gated_body, 0)

    def second_body(m, carry):
        real, imag = forward(m, sig)
        f0r, f0i = spectra_of(m, 0)
        f1r, f1i = spectra_of(m, 1)
        gr, gi, br, bi = real[:, :LANES], imag[:, :LANES], real[:, LANES:], imag[:, LANES:]
        put(m, 0, *complex_product(gr, gi, f1r, f1i))
        put(m, 1, *conj_product(f0r, f0i, br, bi))
        return carry

    lax.fori_loop(0, 2 * length // TILE, second_body, 0)
    inverse(conv2)

    def last_body(c, carry):
        both = conv2[chunk(c), :]
        second, grad_value = both[:, :LANES], both[:, LANES:]
        staged[0, chunk(c), :] = (gates[1, chunk(c), :] * second).astype(BF16)
        cot[2, offset(c, 0), :] = (og[chunk(c), :].astype(F32) * second).astype(BF16).astype(F32)
        cot[0, offset(c, 0), :] = grad_value.astype(BF16).astype(F32)
        return carry

    lax.fori_loop(0, seq, last_body, 0)
    out_layer = exchange(LAYER, lambda d: staged.at[0, rows(d)], layer_out.at[:, lanes(me)])
    close(2)
    close(0)
    grads_of(2, 3)
    out_two = exchange(SG_TWO, lambda d: staged.at[3, rows(d)], stream_grads.at[2, :, lanes(me)])
    grads_of(0, 1)
    out_value = exchange(SG_VALUE, lambda d: staged.at[1, rows(d)], stream_grads.at[0, :, lanes(me)])
    tap_send[pl.ds(9, 7), :] = jnp.zeros((7, LANES), F32)
    out_taps = exchange(TAPS_OUT, lambda d: tap_send, tap_out.at[:, lanes(me)])
    outs = [out_one, out_layer, out_two, out_value, out_taps]
    for exchanged in outs:
        arrive(exchanged)
    for own, copies in sent + outs:
        for copy in copies:
            copy.wait_send()


def moved(streams, short_taps, long_filters, out_grad):
    seq = lax.axis_size("seq")
    streams_count, part_rows, blocks, channels = streams.shape
    part = part_rows * blocks
    length = part * seq
    fwd, inv = dft_tables(blocks, part_rows * seq)
    any_spec = pl.BlockSpec(memory_space=pl.ANY)
    vmem = pl.BlockSpec(memory_space=pltpu.VMEM)
    flat_taps = jnp.pad(short_taps.reshape(9, channels), ((0, 7), (0, 0)))
    slots = 11
    layer, grads, taps = pl.pallas_call(
        functools.partial(kernel, seq, blocks),
        out_shape=(
            jax.ShapeDtypeStruct((part, channels), BF16),
            jax.ShapeDtypeStruct((3, part, channels), BF16),
            jax.ShapeDtypeStruct((16, channels), F32),
        ),
        in_specs=[any_spec, vmem, any_spec, any_spec, any_spec, any_spec],
        out_specs=(any_spec, any_spec, any_spec),
        scratch_shapes=[
            pltpu.VMEM((2 * length, length), BF16),
            pltpu.VMEM((length, 2 * length), BF16),
            pltpu.VMEM((length, 2 * LANES), BF16),
            pltpu.VMEM((3, length, LANES), BF16),
            pltpu.VMEM((length, LANES), BF16),
            pltpu.VMEM((3, length + 2 * blocks, LANES), F32),
            pltpu.VMEM((3, length + 2 * blocks, LANES), F32),
            pltpu.VMEM((2, length, LANES), F32),
            pltpu.VMEM((length, 2 * LANES), BF16),
            pltpu.VMEM((2 * length, 2 * LANES), F32),
            pltpu.VMEM((2 * length, 2 * LANES), BF16),
            pltpu.VMEM((length, 2 * LANES), F32),
            pltpu.VMEM((length, 2 * LANES), F32),
            pltpu.VMEM((4, length, LANES), BF16),
            pltpu.VMEM((16, LANES), F32),
            pltpu.SemaphoreType.DMA((slots, seq)),
            pltpu.SemaphoreType.DMA((slots, seq)),
            pltpu.SemaphoreType.DMA((2,)),
        ],
        compiler_params=pltpu.CompilerParams(
            collective_id=0, has_side_effects=True, vmem_limit_bytes=48 * 1024 * 1024
        ),
    )(
        streams.reshape(3, part, channels),
        flat_taps,
        long_filters.reshape(2, part, channels),
        out_grad.reshape(part, channels),
        jnp.asarray(fwd),
        jnp.asarray(inv),
    )
    return (
        layer.reshape(part_rows, blocks, channels),
        grads.reshape(3, part_rows, blocks, channels),
        taps[:9].reshape(3, 3, channels),
    )


def either(streams, short_taps, long_filters, out_grad):
    seq = lax.axis_size("seq")
    part_rows, blocks, channels = streams.shape[1:]
    length = part_rows * blocks * seq
    fits = (
        channels == LANES * seq
        and blocks == 8
        and part_rows * blocks % LANES == 0
        and length % TILE == 0
        and length <= 1024
    )
    return (moved if fits else local)(streams, short_taps, long_filters, out_grad)


def solution(mesh):
    in_specs = (
        P(None, "seq", "group", "tensor"),
        P(None, None, "tensor"),
        P(None, "seq", None, "tensor"),
        P("seq", "group", "tensor"),
    )
    out_specs = (
        P("seq", "group", "tensor"),
        P(None, "seq", "group", "tensor"),
        P("group", None, "tensor"),
    )
    return jax.shard_map(either, mesh=mesh, in_specs=in_specs, out_specs=out_specs, check_vma=False)
```

profile of v0, /device:TPU:0, one launch (start us, length us, event | category | flops | bytes accessed | tf_op | source)
XLA Modules:
  0.0 76.3 jit_solution(14130894979941046089)
XLA Ops:
  0.6 0.8 %reshape.28 = f32[9,1024]{1,0:T(8,128)S(1)} reshape(f32[3,3,1024]{2,1,0:T(4,128)} %param.7) | data formatting | bytes 73728 | tf_op jit(solution)/shard_map/reshape | solution.py:434
  1.5 0.0 copy-start
  1.5 1.1 %copy-done = bf16[3,16,8,1024]{3,2,1,0:T(8,128)(2,1)S(1)} copy-done((bf16[3,16,8,1024]{3,2,1,0:T(8,128)(2,1)S(1)}, bf16[3,16,8,1024]{3,2,1,0:T(8,128)(2,1)}, u32[]{:S(2)}) %copy-start) | copy-done | bytes 786456
  2.6 0.0 copy-start.1
  2.6 1.0 %copy-done.1 = bf16[2,16,8,1024]{3,2,1,0:T(8,128)(2,1)S(1)} copy-done((bf16[2,16,8,1024]{3,2,1,0:T(8,128)(2,1)S(1)}, bf16[2,16,8,1024]{3,2,1,0:T(8,128)(2,1)}, u32[]{:S(2)}) %copy-start.1) | copy-done | bytes 524312
  3.6 0.0 copy-start.2
  3.6 0.9 %copy-done.2 = bf16[16,8,1024]{2,1,0:T(8,128)(2,1)S(1)} copy-done((bf16[16,8,1024]{2,1,0:T(8,128)(2,1)S(1)}, bf16[16,8,1024]{2,1,0:T(8,128)(2,1)}, u32[]{:S(2)}) %copy-start.2) | copy-done | bytes 262168
  4.6 69.4 %shard_map.85 = (bf16[128,1024]{1,0:T(8,128)(2,1)S(1)}, bf16[3,128,1024]{2,1,0:T(8,128)(2,1)S(1)}, f32[16,1024]{1,0:T(8,128)S(1)}) custom-call(bf16[3,128,1024]{2,1,0:T(8,128)(2,1)S(1)} %bitcast.6, f32[16,1024]{1,0:T(8,128)S(1)} %pad.4.taps, bf16[2,128,1024]{2,1,0:T(8,128)(2,1)S(1)} %bitcast.8, bf16[128,1024]{1,0:T(8,128)(2,1)S(1)} %bitcast.9, ...), custom_call_target="tpu_custom_call" | custom-call | tf_op jit(solution)/shard_map/pallas_call | solution.py:436
  74.0 0.6 reshape.33
  74.7 0.7 copy.11
  75.4 0.9 %copy.12 = bf16[3,16,8,1024]{3,2,1,0:T(8,128)(2,1)} copy(bf16[3,16,8,1024]{3,2,1,0:T(8,128)(2,1)S(1)} %bitcast.7) | data formatting | bytes 1572864
  (1 shorter events, 0.0 us)
Async XLA Ops:
  1.5 1.1 %copy-start = (bf16[3,16,8,1024]{3,2,1,0:T(8,128)(2,1)S(1)}, bf16[3,16,8,1024]{3,2,1,0:T(8,128)(2,1)}, u32[]{:S(2)}) copy-start(bf16[3,16,8,1024]{3,2,1,0:T(8,128)(2,1)} %param.6) | copy-start | bytes 2359300
  2.6 1.0 %copy-start.1 = (bf16[2,16,8,1024]{3,2,1,0:T(8,128)(2,1)S(1)}, bf16[2,16,8,1024]{3,2,1,0:T(8,128)(2,1)}, u32[]{:S(2)}) copy-start(bf16[2,16,8,1024]{3,2,1,0:T(8,128)(2,1)} %param.8) | copy-start | bytes 1572868
  3.6 0.9 %copy-start.2 = (bf16[16,8,1024]{2,1,0:T(8,128)(2,1)S(1)}, bf16[16,8,1024]{2,1,0:T(8,128)(2,1)}, u32[]{:S(2)}) copy-start(bf16[16,8,1024]{2,1,0:T(8,128)(2,1)} %param.9) | copy-start | bytes 786436
where the time goes:
time: 76.6 us; the launch traced here: 76.3 us
  Pallas kernels  69.4 us (91%)
  local copies, waits for them, and re-layouts  6.17 us (8%)
    pallas_call x1, Pallas kernels, moved(): pl.pallas_call(functools.partial(kernel, seq, blocks), out_shape=(jax.Sha...  69.4 us
    unnamed x8, local copies, waits for them, and re-layouts  4.7 us

commit v1 on v0

--- a/solution.py
+++ b/solution.py
@@ -161,6 +161,12 @@
     return (layer_out, stream_grads, tap_total * (1.0 / math.sqrt(block_rows * seq_count)))
 
 
+def split_table(table):
+    high = table.astype(ml_dtypes.bfloat16)
+    low = (table - high.astype(np.float64)).astype(ml_dtypes.bfloat16)
+    return np.stack([high, low])
+
+
 def dft_tables(blocks, rows):
     length = blocks * rows
     place = np.arange(length)
@@ -169,10 +175,7 @@
     freq = np.arange(length).reshape(-1, half)
     angle = ((2 * freq[:, :, None] + 1) * time[None, None, :] % (4 * length)) * (math.pi / (2 * length))
     table = np.concatenate([np.cos(angle), -np.sin(angle)], axis=1).reshape(2 * length, length)
-    return (
-        table.astype(ml_dtypes.bfloat16),
-        np.ascontiguousarray(table.T / length).astype(ml_dtypes.bfloat16),
-    )
+    return split_table(table), split_table(table.T / length)
 
 
 FILTER0, FILTER1, VALUE, GATE_TWO, OUT_GRAD, GATE_ONE, SG_ONE, LAYER, SG_TWO, SG_VALUE, TAPS_OUT = range(11)
@@ -181,10 +184,12 @@
 def kernel(
     seq, blocks, streams, taps, filters, out_grad, fwd_hbm, inv_hbm,
     layer_out, stream_grads, tap_out,
-    fwd, inv, xf, sb, og, s32, cot, gates, sig, spec_f, prod, conv, conv2, staged, tap_send,
+    fwd, inv, xf, sb, og, s32, cot, gates, sig, sig_low, spec_f, prod, prod_low, conv, conv2, staged, tap_send,
     send_sem, recv_sem, table_sem,
 ):
     me = lax.axis_index("seq")
+    group = lax.axis_index("group")
+    other = 1 - group
     part = streams.shape[1]
     length = part * seq
     half = TILE // 2
@@ -222,26 +227,30 @@
     barrier = pltpu.get_barrier_semaphore()
     for k in range(1, seq):
         pl.semaphore_signal(barrier, inc=1, device_id={"seq": peer(k)}, device_id_type=MESH)
+    pl.semaphore_signal(barrier, inc=1, device_id={"group": other}, device_id_type=MESH)
     fwd_copy = pltpu.make_async_copy(fwd_hbm, fwd, table_sem.at[0])
     inv_copy = pltpu.make_async_copy(inv_hbm, inv, table_sem.at[1])
+    pl.semaphore_wait(barrier, seq)
+
+    mine = rows(me)
+    in_f = exchange(FILTER0, lambda d: filters.at[group, :, lanes(d)], xf.at[mine, lanes(group)])
+    own_f1 = pltpu.make_async_copy(
+        filters.at[other, :, lanes(me)], xf.at[mine, lanes(other)], recv_sem.at[FILTER1, 0]
+    )
+    own_f1.start()
     fwd_copy.start()
-    inv_copy.start()
-    pl.semaphore_wait(barrier, seq - 1)
-
-    mine = rows(me)
-    in_f0 = exchange(FILTER0, lambda d: filters.at[0, :, lanes(d)], xf.at[mine, pl.ds(0, LANES)])
-    in_f1 = exchange(FILTER1, lambda d: filters.at[1, :, lanes(d)], xf.at[mine, pl.ds(LANES, LANES)])
     in_v = exchange(VALUE, lambda d: streams.at[0, :, lanes(d)], sb.at[0, mine])
     in_g2 = exchange(GATE_TWO, lambda d: streams.at[2, :, lanes(d)], sb.at[2, mine])
     in_og = exchange(OUT_GRAD, lambda d: out_grad.at[:, lanes(d)], og.at[mine])
     in_g1 = exchange(GATE_ONE, lambda d: streams.at[1, :, lanes(d)], sb.at[1, mine])
-    sent = [in_f0, in_f1, in_v, in_g2, in_og, in_g1]
+    inv_copy.start()
+    sent = [in_f, in_v, in_g2, in_og, in_g1]
 
     pad = 2 * blocks
     sub = lax.broadcasted_iota(jnp.int32, (blocks, LANES), 0)
 
     def tap(s, j):
-        return taps[pl.ds(3 * s + j, 1), lanes(me)]
+        return taps[s, pl.ds(j, 1), lanes(me)]
 
     def chunk(c):
         return pl.ds(pl.multiple_of(c * part, part), part)
@@ -278,8 +287,14 @@
             )
 
     def grads_of(s, slot):
+        def body(c, carry):
+            staged[slot, chunk(c), :] = cots(s, c)
+            return carry
+
+        lax.fori_loop(0, seq, body, 0)
+
+    def taps_of(s):
         def body(c, sums):
-            staged[slot, chunk(c), :] = cots(s, c)
             now = cot[s, offset(c, 0), :]
             return tuple(
                 sums[j]
@@ -291,7 +306,7 @@
 
         sums = lax.fori_loop(0, seq, body, tuple(jnp.zeros((8, LANES), F32) for _ in range(3)))
         for j in range(3):
-            tap_send[pl.ds(3 * s + j, 1), :] = jnp.sum(sums[j], axis=0, keepdims=True) * (
+            tap_send[s, pl.ds(j, 1), :] = jnp.sum(sums[j], axis=0, keepdims=True) * (
                 1.0 / math.sqrt(length)
             )
 
@@ -299,7 +314,7 @@
         return pl.ds(pl.multiple_of(m * TILE, TILE), TILE)
 
     def forward(m, signals):
-        out = jnp.dot(fwd[tile(m), :], signals[...], preferred_element_type=F32)
+        out = jnp.dot(fwd[0, tile(m), :], signals[...], preferred_element_type=F32)
         return out[:half], out[half:]
 
     def put(m, col, real, imag):
@@ -313,19 +328,40 @@
             spec_f[pl.ds(pl.multiple_of(m * TILE + half, half), half), cols],
         )
 
-    def inverse(into):
+    def put_low(m, col, real, imag):
+        for start, value in ((0, real), (half, imag)):
+            low = (value - value.astype(BF16).astype(F32)).astype(BF16)
+            prod_low[pl.ds(pl.multiple_of(m * TILE + start, half), half), col * LANES:(col + 1) * LANES] = low
+
+    def inverse(into, split):
         def body(m, carry):
-            into[tile(m), :] = jnp.dot(inv[tile(m), :], prod[...], preferred_element_type=F32)
+            out = jnp.dot(inv[0, tile(m), :], prod[...], preferred_element_type=F32)
+            if split:
+                out = out + jnp.dot(inv[1, tile(m), :], prod[...], preferred_element_type=F32)
+                out = out + jnp.dot(inv[0, tile(m), :], prod_low[...], preferred_element_type=F32)
+            into[tile(m), :] = out
             return carry
 
         lax.fori_loop(0, length // TILE, body, 0)
 
+    in_f[0].wait()
+    handed = []
+    for k, copy in zip(order, in_f[1]):
+        copy.wait_recv()
+        piece = xf.at[rows(lax.rem(me - k + seq, seq)), lanes(group)]
+        hand = pltpu.make_async_remote_copy(
+            src_ref=piece, dst_ref=piece, send_sem=send_sem.at[FILTER1, k],
+            recv_sem=recv_sem.at[FILTER1, k], device_id={"group": other}, device_id_type=MESH,
+        )
+        hand.start()
+        handed.append(hand)
+    sent.append((own_f1, handed))
+    arrive((own_f1, handed))
     fwd_copy.wait()
-    arrive(in_f0)
-    arrive(in_f1)
 
     def filter_body(m, carry):
-        spec_f[tile(m), :] = jnp.dot(fwd[tile(m), :], xf[...], preferred_element_type=F32)
+        out = jnp.dot(fwd[0, tile(m), :], xf[...], preferred_element_type=F32)
+        spec_f[tile(m), :] = out + jnp.dot(fwd[1, tile(m), :], xf[...], preferred_element_type=F32)
         return carry
 
     lax.fori_loop(0, 2 * length // TILE, filter_body, 0)
@@ -346,23 +382,31 @@
     def back_body(c, carry):
         gate = filtered(2, c)
         gates[1, chunk(c), :] = gate.astype(F32)
-        sig[chunk(c), LANES:] = (og[chunk(c), :].astype(F32) * gate.astype(F32)).astype(BF16)
+        back = og[chunk(c), :].astype(F32) * gate.astype(F32)
+        sig[chunk(c), LANES:] = back.astype(BF16)
+        sig_low[chunk(c), :] = (back - back.astype(BF16).astype(F32)).astype(BF16)
         return carry
 
     lax.fori_loop(0, seq, back_body, 0)
 
     def first_body(m, carry):
-        real, imag = forward(m, sig)
+        out = jnp.dot(fwd[0, tile(m), :], sig[...], preferred_element_type=F32)
+        out = out + jnp.dot(fwd[1, tile(m), :], sig[...], preferred_element_type=F32)
+        low = jnp.dot(fwd[0, tile(m), :], sig_low[...], preferred_element_type=F32)
+        back = out[:, LANES:] + low
         f0r, f0i = spectra_of(m, 0)
         f1r, f1i = spectra_of(m, 1)
-        vr, vi, br, bi = real[:, :LANES], imag[:, :LANES], real[:, LANES:], imag[:, LANES:]
-        put(m, 0, *complex_product(vr, vi, f0r, f0i))
-        put(m, 1, *conj_product(f1r, f1i, br, bi))
+        first = complex_product(out[:half, :LANES], out[half:, :LANES], f0r, f0i)
+        second = conj_product(f1r, f1i, back[:half], back[half:])
+        put(m, 0, *first)
+        put_low(m, 0, *first)
+        put(m, 1, *second)
+        put_low(m, 1, *second)
         return carry
 
     lax.fori_loop(0, 2 * length // TILE, first_body, 0)
     inv_copy.wait()
-    inverse(conv)
+    inverse(conv, True)
 
     def one_body(c, carry):
         both = conv[chunk(c), :]
@@ -371,10 +415,10 @@
 
     lax.fori_loop(0, seq, one_body, 0)
     close(1)
+    grads_of(1, 2)
+    out_one = exchange(SG_ONE, lambda d: staged.at[2, rows(d)], stream_grads.at[1, :, lanes(me)])
     arrive(in_g1)
     widen(1)
-    grads_of(1, 2)
-    out_one = exchange(SG_ONE, lambda d: staged.at[2, rows(d)], stream_grads.at[1, :, lanes(me)])
 
     def gated_body(c, carry):
         gate = filtered(1, c).astype(F32)
@@ -395,7 +439,7 @@
         return carry
 
     lax.fori_loop(0, 2 * length // TILE, second_body, 0)
-    inverse(conv2)
+    inverse(conv2, False)
 
     def last_body(c, carry):
         both = conv2[chunk(c), :]
@@ -413,8 +457,9 @@
     out_two = exchange(SG_TWO, lambda d: staged.at[3, rows(d)], stream_grads.at[2, :, lanes(me)])
     grads_of(0, 1)
     out_value = exchange(SG_VALUE, lambda d: staged.at[1, rows(d)], stream_grads.at[0, :, lanes(me)])
-    tap_send[pl.ds(9, 7), :] = jnp.zeros((7, LANES), F32)
-    out_taps = exchange(TAPS_OUT, lambda d: tap_send, tap_out.at[:, lanes(me)])
+    for s in range(3):
+        taps_of(s)
+    out_taps = exchange(TAPS_OUT, lambda d: tap_send, tap_out.at[:, :, lanes(me)])
     outs = [out_one, out_layer, out_two, out_value, out_taps]
     for exchanged in outs:
         arrive(exchanged)
@@ -430,21 +475,21 @@
     length = part * seq
     fwd, inv = dft_tables(blocks, part_rows * seq)
     any_spec = pl.BlockSpec(memory_space=pl.ANY)
+    hbm = pl.BlockSpec(memory_space=pltpu.HBM)
     vmem = pl.BlockSpec(memory_space=pltpu.VMEM)
-    flat_taps = jnp.pad(short_taps.reshape(9, channels), ((0, 7), (0, 0)))
     slots = 11
     layer, grads, taps = pl.pallas_call(
         functools.partial(kernel, seq, blocks),
         out_shape=(
             jax.ShapeDtypeStruct((part, channels), BF16),
             jax.ShapeDtypeStruct((3, part, channels), BF16),
-            jax.ShapeDtypeStruct((16, channels), F32),
+            jax.ShapeDtypeStruct((3, 3, channels), F32),
         ),
-        in_specs=[any_spec, vmem, any_spec, any_spec, any_spec, any_spec],
+        in_specs=[hbm, vmem, hbm, hbm, hbm, hbm],
         out_specs=(any_spec, any_spec, any_spec),
         scratch_shapes=[
-            pltpu.VMEM((2 * length, length), BF16),
-            pltpu.VMEM((length, 2 * length), BF16),
+            pltpu.VMEM((2, 2 * length, length), BF16),
+            pltpu.VMEM((2, length, 2 * length), BF16),
             pltpu.VMEM((length, 2 * LANES), BF16),
             pltpu.VMEM((3, length, LANES), BF16),
             pltpu.VMEM((length, LANES), BF16),
@@ -452,12 +497,14 @@
             pltpu.VMEM((3, length + 2 * blocks, LANES), F32),
             pltpu.VMEM((2, length, LANES), F32),
             pltpu.VMEM((length, 2 * LANES), BF16),
+            pltpu.VMEM((length, LANES), BF16),
             pltpu.VMEM((2 * length, 2 * LANES), F32),
+            pltpu.VMEM((2 * length, 2 * LANES), BF16),
             pltpu.VMEM((2 * length, 2 * LANES), BF16),
             pltpu.VMEM((length, 2 * LANES), F32),
             pltpu.VMEM((length, 2 * LANES), F32),
             pltpu.VMEM((4, length, LANES), BF16),
-            pltpu.VMEM((16, LANES), F32),
+            pltpu.VMEM((3, 3, LANES), F32),
             pltpu.SemaphoreType.DMA((slots, seq)),
             pltpu.SemaphoreType.DMA((slots, seq)),
             pltpu.SemaphoreType.DMA((2,)),
@@ -467,7 +514,7 @@
         ),
     )(
         streams.reshape(3, part, channels),
-        flat_taps,
+        short_taps,
         long_filters.reshape(2, part, channels),
         out_grad.reshape(part, channels),
         jnp.asarray(fwd),
@@ -476,7 +523,7 @@
     return (
         layer.reshape(part_rows, blocks, channels),
         grads.reshape(3, part_rows, blocks, channels),
-        taps[:9].reshape(3, 3, channels),
+        taps,
     )
 
 
@@ -486,6 +533,7 @@
     length = part_rows * blocks * seq
     fits = (
         channels == LANES * seq
+        and lax.axis_size("group") == 2
         and blocks == 8
         and part_rows * blocks % LANES == 0
         and length % TILE == 0

time: 76.6 us -> 74.9 us (0.978)
  Pallas kernels: 69.4 us -> 67.8 us
    pallas_call x1, Pallas kernels: 69.4 us -> 67.8 us  [moved(): pl.pallas_call(functools.partial(kernel, seq, blocks), out_shape=(jax.Sha...]
    reshape x2 -> x0, local copies, waits for them, and re-layouts: 1.46 us -> none  [the longest x1 0.82 us: moved(): flat_taps = jnp.pad(short_taps.reshape(9, channels), ((0, 7), (0, 0)))]
    unnamed x8 -> x11, local copies, waits for them, and re-layouts: 4.7 us -> 6.12 us
where the time goes in v1:
time: 74.9 us; the launch traced here: 74.6 us
  Pallas kernels  67.8 us (91%)
  local copies, waits for them, and re-layouts  6.12 us (8%)
    pallas_call x1, Pallas kernels, moved(): pl.pallas_call(functools.partial(kernel, seq, blocks), out_shape=(jax.Sha...  67.8 us
    unnamed x11, local copies, waits for them, and re-layouts  6.12 us

profile of v1, /device:TPU:0, one launch (start us, length us, event | category | flops | bytes accessed | tf_op | source)
XLA Modules:
  0.0 74.6 jit_solution(16113533371086872481)
XLA Ops:
  0.6 0.0 copy-start
  0.6 1.1 %copy-done = bf16[3,16,8,1024]{3,2,1,0:T(8,128)(2,1)S(1)} copy-done((bf16[3,16,8,1024]{3,2,1,0:T(8,128)(2,1)S(1)}, bf16[3,16,8,1024]{3,2,1,0:T(8,128)(2,1)}, u32[]{:S(2)}) %copy-start) | copy-done | bytes 786456
  1.8 0.0 copy-start.1
  1.8 1.0 %copy-done.1 = bf16[2,16,8,1024]{3,2,1,0:T(8,128)(2,1)S(1)} copy-done((bf16[2,16,8,1024]{3,2,1,0:T(8,128)(2,1)S(1)}, bf16[2,16,8,1024]{3,2,1,0:T(8,128)(2,1)}, u32[]{:S(2)}) %copy-start.1) | copy-done | bytes 524312
  2.8 0.0 copy-start.2
  2.8 0.9 %copy-done.2 = bf16[16,8,1024]{2,1,0:T(8,128)(2,1)S(1)} copy-done((bf16[16,8,1024]{2,1,0:T(8,128)(2,1)S(1)}, bf16[16,8,1024]{2,1,0:T(8,128)(2,1)}, u32[]{:S(2)}) %copy-start.2) | copy-done | bytes 262168
  3.8 0.0 copy-start.3
  3.8 0.8 %copy-done.3 = f32[3,3,1024]{2,1,0:T(4,128)S(1)} copy-done((f32[3,3,1024]{2,1,0:T(4,128)S(1)}, f32[3,3,1024]{2,1,0:T(4,128)}, u32[]{:S(2)}) %copy-start.3) | copy-done | bytes 36888
  4.6 67.8 %shard_map.85 = (bf16[128,1024]{1,0:T(8,128)(2,1)S(1)}, bf16[3,128,1024]{2,1,0:T(8,128)(2,1)S(1)}, f32[3,3,1024]{2,1,0:T(4,128)S(1)}) custom-call(bf16[3,128,1024]{2,1,0:T(8,128)(2,1)S(1)} %bitcast.6, f32[3,3,1024]{2,1,0:T(4,128)S(1)} %copy-done.3, bf16[2,128,1024]{2,1,0:T(8,128)(2,1)S(1)} %bitcast.7, bf16[128,1024]{1,0:T(8,128)(2,1)S(1)} %bitcast.9, ...), custom_call_target="tpu_custom_call" | custom-call | tf_op jit(solution)/shard_map/pallas_call | solution.py:481
  72.4 0.7 copy.12
  73.1 0.9 %copy.13 = bf16[3,16,8,1024]{3,2,1,0:T(8,128)(2,1)} copy(bf16[3,16,8,1024]{3,2,1,0:T(8,128)(2,1)S(1)} %bitcast.5) | data formatting | bytes 1572864
  74.0 0.6 copy.14
Async XLA Ops:
  0.6 1.1 %copy-start = (bf16[3,16,8,1024]{3,2,1,0:T(8,128)(2,1)S(1)}, bf16[3,16,8,1024]{3,2,1,0:T(8,128)(2,1)}, u32[]{:S(2)}) copy-start(bf16[3,16,8,1024]{3,2,1,0:T(8,128)(2,1)} %param.6) | copy-start | bytes 2359300
  1.8 1.0 %copy-start.1 = (bf16[2,16,8,1024]{3,2,1,0:T(8,128)(2,1)S(1)}, bf16[2,16,8,1024]{3,2,1,0:T(8,128)(2,1)}, u32[]{:S(2)}) copy-start(bf16[2,16,8,1024]{3,2,1,0:T(8,128)(2,1)} %param.8) | copy-start | bytes 1572868
  2.8 0.9 %copy-start.2 = (bf16[16,8,1024]{2,1,0:T(8,128)(2,1)S(1)}, bf16[16,8,1024]{2,1,0:T(8,128)(2,1)}, u32[]{:S(2)}) copy-start(bf16[16,8,1024]{2,1,0:T(8,128)(2,1)} %param.9) | copy-start | bytes 786436
  3.8 0.8 %copy-start.3 = (f32[3,3,1024]{2,1,0:T(4,128)S(1)}, f32[3,3,1024]{2,1,0:T(4,128)}, u32[]{:S(2)}) copy-start(f32[3,3,1024]{2,1,0:T(4,128)} %taps.1) | copy-start | bytes 110596

commit v2 on v1

--- a/solution.py
+++ b/solution.py
@@ -184,7 +184,7 @@
 def kernel(
     seq, blocks, streams, taps, filters, out_grad, fwd_hbm, inv_hbm,
     layer_out, stream_grads, tap_out,
-    fwd, inv, xf, sb, og, s32, cot, gates, sig, sig_low, spec_f, prod, prod_low, conv, conv2, staged, tap_send,
+    fwd, inv, xf, sb, og, s32, cot, gates, sig, sig_low, spec_f, prod, conv, conv2, staged, tap_send,
     send_sem, recv_sem, table_sem,
 ):
     me = lax.axis_index("seq")
@@ -328,17 +328,11 @@
             spec_f[pl.ds(pl.multiple_of(m * TILE + half, half), half), cols],
         )
 
-    def put_low(m, col, real, imag):
-        for start, value in ((0, real), (half, imag)):
-            low = (value - value.astype(BF16).astype(F32)).astype(BF16)
-            prod_low[pl.ds(pl.multiple_of(m * TILE + start, half), half), col * LANES:(col + 1) * LANES] = low
-
     def inverse(into, split):
         def body(m, carry):
             out = jnp.dot(inv[0, tile(m), :], prod[...], preferred_element_type=F32)
             if split:
                 out = out + jnp.dot(inv[1, tile(m), :], prod[...], preferred_element_type=F32)
-                out = out + jnp.dot(inv[0, tile(m), :], prod_low[...], preferred_element_type=F32)
             into[tile(m), :] = out
             return carry
 
@@ -399,9 +393,7 @@
         first = complex_product(out[:half, :LANES], out[half:, :LANES], f0r, f0i)
         second = conj_product(f1r, f1i, back[:half], back[half:])
         put(m, 0, *first)
-        put_low(m, 0, *first)
         put(m, 1, *second)
-        put_low(m, 1, *second)
         return carry
 
     lax.fori_loop(0, 2 * length // TILE, first_body, 0)
@@ -500,7 +492,6 @@
             pltpu.VMEM((length, LANES), BF16),
             pltpu.VMEM((2 * length, 2 * LANES), F32),
             pltpu.VMEM((2 * length, 2 * LANES), BF16),
-            pltpu.VMEM((2 * length, 2 * LANES), BF16),
             pltpu.VMEM((length, 2 * LANES), F32),
             pltpu.VMEM((length, 2 * LANES), F32),
             pltpu.VMEM((4, length, LANES), BF16),
@@ -513,10 +504,10 @@
             collective_id=0, has_side_effects=True, vmem_limit_bytes=48 * 1024 * 1024
         ),
     )(
-        streams.reshape(3, part, channels),
+        pltpu.with_memory_space_constraint(streams.reshape(3, part, channels), pltpu.HBM),
         short_taps,
-        long_filters.reshape(2, part, channels),
-        out_grad.reshape(part, channels),
+        pltpu.with_memory_space_constraint(long_filters.reshape(2, part, channels), pltpu.HBM),
+        pltpu.with_memory_space_constraint(out_grad.reshape(part, channels), pltpu.HBM),
         jnp.asarray(fwd),
         jnp.asarray(inv),
     )

time: 74.9 us -> 70.4 us (0.940)
  local copies, waits for them, and re-layouts: 6.12 us -> 3 us
  Pallas kernels: 67.8 us -> 66.6 us
    unnamed x11 -> x5, local copies, waits for them, and re-layouts: 6.12 us -> 3 us
    pallas_call x1, Pallas kernels: 67.8 us -> 66.6 us  [moved(): pl.pallas_call(functools.partial(kernel, seq, blocks), out_shape=(jax.Sha...]
where the time goes in v2:
time: 70.4 us; the launch traced here: 70.3 us
  Pallas kernels  66.6 us (95%)
  local copies, waits for them, and re-layouts  3 us (4%)
    pallas_call x1, Pallas kernels, moved(): pl.pallas_call(functools.partial(kernel, seq, blocks), out_shape=(jax.Sha...  66.6 us
    unnamed x5, local copies, waits for them, and re-layouts  3 us

profile of v2, /device:TPU:0, one launch (start us, length us, event | category | flops | bytes accessed | tf_op | source)
XLA Modules:
  0.0 70.3 jit_solution(14360922818612391703)
XLA Ops:
  0.6 0.0 copy-start
  0.6 0.8 %copy-done = f32[3,3,1024]{2,1,0:T(4,128)S(1)} copy-done((f32[3,3,1024]{2,1,0:T(4,128)S(1)}, f32[3,3,1024]{2,1,0:T(4,128)}, u32[]{:S(2)}) %copy-start) | copy-done | bytes 36888
  1.4 66.6 %shard_map.85 = (bf16[128,1024]{1,0:T(8,128)(2,1)S(1)}, bf16[3,128,1024]{2,1,0:T(8,128)(2,1)S(1)}, f32[3,3,1024]{2,1,0:T(4,128)S(1)}) custom-call(bf16[3,128,1024]{2,1,0:T(8,128)(2,1)} %bitcast.7, f32[3,3,1024]{2,1,0:T(4,128)S(1)} %copy-done, bf16[2,128,1024]{2,1,0:T(8,128)(2,1)} %bitcast.8, bf16[128,1024]{1,0:T(8,128)(2,1)} %bitcast.9, ...), custom_call_target="tpu_custom_call" | custom-call | tf_op jit(solution)/shard_map/pallas_call | solution.py:473
  68.1 0.7 %copy.12 = bf16[16,8,1024]{2,1,0:T(8,128)(2,1)} copy(bf16[16,8,1024]{2,1,0:T(8,128)(2,1)S(1)} %bitcast.6) | data formatting | bytes 524288
  68.8 0.9 %copy.13 = bf16[3,16,8,1024]{3,2,1,0:T(8,128)(2,1)} copy(bf16[3,16,8,1024]{3,2,1,0:T(8,128)(2,1)S(1)} %bitcast.5) | data formatting | bytes 1572864
  69.6 0.6 copy.14
Async XLA Ops:
  0.6 0.8 %copy-start = (f32[3,3,1024]{2,1,0:T(4,128)S(1)}, f32[3,3,1024]{2,1,0:T(4,128)}, u32[]{:S(2)}) copy-start(f32[3,3,1024]{2,1,0:T(4,128)} %taps.1) | copy-start | bytes 110596

commit v3 on v2

--- a/solution.py
+++ b/solution.py
@@ -263,7 +263,7 @@
             s32[s, offset(c, pad), :] = sb[s, chunk(c), :].astype(F32)
             return carry
 
-        lax.fori_loop(0, seq, body, 0)
+        lax.fori_loop(0, seq, body, 0, unroll=4)
         for step in range(2):
             edge = s32[s, pl.ds(length + step * blocks, blocks), :]
             s32[s, pl.ds(step * blocks, blocks), :] = jnp.where(sub == 0, 0.0, pltpu.roll(edge, 1, 0))
@@ -291,7 +291,7 @@
             staged[slot, chunk(c), :] = cots(s, c)
             return carry
 
-        lax.fori_loop(0, seq, body, 0)
+        lax.fori_loop(0, seq, body, 0, unroll=4)
 
     def taps_of(s):
         def body(c, sums):
@@ -304,7 +304,7 @@
                 for j in range(3)
             )
 
-        sums = lax.fori_loop(0, seq, body, tuple(jnp.zeros((8, LANES), F32) for _ in range(3)))
+        sums = lax.fori_loop(0, seq, body, tuple(jnp.zeros((8, LANES), F32) for _ in range(3)), unroll=4)
         for j in range(3):
             tap_send[s, pl.ds(j, 1), :] = jnp.sum(sums[j], axis=0, keepdims=True) * (
                 1.0 / math.sqrt(length)
@@ -336,7 +336,7 @@
             into[tile(m), :] = out
             return carry
 
-        lax.fori_loop(0, length // TILE, body, 0)
+        lax.fori_loop(0, length // TILE, body, 0, unroll=4)
 
     in_f[0].wait()
     handed = []
@@ -358,7 +358,7 @@
         spec_f[tile(m), :] = out + jnp.dot(fwd[1, tile(m), :], xf[...], preferred_element_type=F32)
         return carry
 
-    lax.fori_loop(0, 2 * length // TILE, filter_body, 0)
+    lax.fori_loop(0, 2 * length // TILE, filter_body, 0, unroll=4)
 
     arrive(in_v)
     widen(0)
@@ -367,7 +367,7 @@
         sig[chunk(c), 0:LANES] = filtered(0, c)
         return carry
 
-    lax.fori_loop(0, seq, value_body, 0)
+    lax.fori_loop(0, seq, value_body, 0, unroll=4)
     arrive(in_g2)
     widen(2)
 
@@ -381,7 +381,7 @@
         sig_low[chunk(c), :] = (back - back.astype(BF16).astype(F32)).astype(BF16)
         return carry
 
-    lax.fori_loop(0, seq, back_body, 0)
+    lax.fori_loop(0, seq, back_body, 0, unroll=4)
 
     def first_body(m, carry):
         out = jnp.dot(fwd[0, tile(m), :], sig[...], preferred_element_type=F32)
@@ -396,7 +396,7 @@
         put(m, 1, *second)
         return carry
 
-    lax.fori_loop(0, 2 * length // TILE, first_body, 0)
+    lax.fori_loop(0, 2 * length // TILE, first_body, 0, unroll=4)
     inv_copy.wait()
     inverse(conv, True)
 
@@ -405,7 +405,7 @@
         cot[1, offset(c, 0), :] = (both[:, LANES:] * both[:, :LANES]).astype(BF16).astype(F32)
         return carry
 
-    lax.fori_loop(0, seq, one_body, 0)
+    lax.fori_loop(0, seq, one_body, 0, unroll=4)
     close(1)
     grads_of(1, 2)
     out_one = exchange(SG_ONE, lambda d: staged.at[2, rows(d)], stream_grads.at[1, :, lanes(me)])
@@ -419,7 +419,7 @@
         sig[chunk(c), LANES:] = (gate * both[:, LANES:]).astype(BF16)
         return carry
 
-    lax.fori_loop(0, seq, gated_body, 0)
+    lax.fori_loop(0, seq, gated_body, 0, unroll=4)
 
     def second_body(m, carry):
         real, imag = forward(m, sig)
@@ -430,7 +430,7 @@
         put(m, 1, *conj_product(f0r, f0i, br, bi))
         return carry
 
-    lax.fori_loop(0, 2 * length // TILE, second_body, 0)
+    lax.fori_loop(0, 2 * length // TILE, second_body, 0, unroll=4)
     inverse(conv2, False)
 
     def last_body(c, carry):
@@ -441,7 +441,7 @@
         cot[0, offset(c, 0), :] = grad_value.astype(BF16).astype(F32)
         return carry
 
-    lax.fori_loop(0, seq, last_body, 0)
+    lax.fori_loop(0, seq, last_body, 0, unroll=4)
     out_layer = exchange(LAYER, lambda d: staged.at[0, rows(d)], layer_out.at[:, lanes(me)])
     close(2)
     close(0)

time: 70.4 us -> 68.8 us (0.977)
  Pallas kernels: 66.6 us -> 65 us
    pallas_call x1, Pallas kernels: 66.6 us -> 65 us  [moved(): pl.pallas_call(functools.partial(kernel, seq, blocks), out_shape=(jax.Sha...]
where the time goes in v3:
time: 68.8 us; the launch traced here: 68.6 us
  Pallas kernels  65 us (94%)
  local copies, waits for them, and re-layouts  3 us (4%)
    pallas_call x1, Pallas kernels, moved(): pl.pallas_call(functools.partial(kernel, seq, blocks), out_shape=(jax.Sha...  65 us
    unnamed x5, local copies, waits for them, and re-layouts  3 us

profile of v3, /device:TPU:0, one launch (start us, length us, event | category | flops | bytes accessed | tf_op | source)
XLA Modules:
  0.0 68.6 jit_solution(1820450259336036280)
XLA Ops:
  0.6 0.0 copy-start
  0.6 0.8 %copy-done = f32[3,3,1024]{2,1,0:T(4,128)S(1)} copy-done((f32[3,3,1024]{2,1,0:T(4,128)S(1)}, f32[3,3,1024]{2,1,0:T(4,128)}, u32[]{:S(2)}) %copy-start) | copy-done | bytes 36888
  1.4 65.0 %shard_map.85 = (bf16[128,1024]{1,0:T(8,128)(2,1)S(1)}, bf16[3,128,1024]{2,1,0:T(8,128)(2,1)S(1)}, f32[3,3,1024]{2,1,0:T(4,128)S(1)}) custom-call(bf16[3,128,1024]{2,1,0:T(8,128)(2,1)} %bitcast.7, f32[3,3,1024]{2,1,0:T(4,128)S(1)} %copy-done, bf16[2,128,1024]{2,1,0:T(8,128)(2,1)} %bitcast.8, bf16[128,1024]{1,0:T(8,128)(2,1)} %bitcast.9, ...), custom_call_target="tpu_custom_call" | custom-call | tf_op jit(solution)/shard_map/pallas_call | solution.py:473
  66.4 0.7 %copy.12 = bf16[16,8,1024]{2,1,0:T(8,128)(2,1)} copy(bf16[16,8,1024]{2,1,0:T(8,128)(2,1)S(1)} %bitcast.6) | data formatting | bytes 524288
  67.1 0.9 %copy.13 = bf16[3,16,8,1024]{3,2,1,0:T(8,128)(2,1)} copy(bf16[3,16,8,1024]{3,2,1,0:T(8,128)(2,1)S(1)} %bitcast.5) | data formatting | bytes 1572864
  68.0 0.6 copy.14
Async XLA Ops:
  0.6 0.8 %copy-start = (f32[3,3,1024]{2,1,0:T(4,128)S(1)}, f32[3,3,1024]{2,1,0:T(4,128)}, u32[]{:S(2)}) copy-start(f32[3,3,1024]{2,1,0:T(4,128)} %taps.1) | copy-start | bytes 110596
